TPU v7x, 32 devices: a whole 2x2x4 slice. The times are simulated.
32 devices in a mesh: patch: 8 (over z, x), frame: 4 (over y, core).
Axes of the slice: x: 2, y: 2, z: 4, core: 2. Of those that a mesh axis runs over, the one named last changes fastest.
Arguments:
- screens: float32 [2, 512, 4096], P(None, 'patch'), may hold values from -6 to 6
- row_offsets: int32 [4, 2, 8], replicated, may hold values from 0 to 256
- col_offsets: int32 [4, 2, 8], replicated, may hold values from 0 to 3840
- amplitude: float32 [256, 256], replicated, may hold values from 0.5 to 1.5
- object_strip: float32 [384, 2048], P(None, 'patch'), may hold values from 0.5 to 1.5
- observed: float32 [4, 256, 2048], P('frame', None, 'patch'), may hold values from 0.5 to 1.5
Outputs:
- screen_grad: float32 [2, 512, 4096], P(None, 'patch', 'frame')
All inputs are finite; a program needn't handle non-finite values.
Results may differ from a plain program's by a relative error of at most 0.0003.
Values sent between devices are 32-bit elements; how exact they have to be, the bound alone decides.
A program may use at most 128 MiB of HBM per device.

v0:
```python
import math

import jax
import jax.numpy as jnp
from jax import lax
from jax.sharding import PartitionSpec as P

CORE = 256
HALO = 64


def padded(cells, sides, width):
    for axis, dim in sides:
        count = lax.axis_size(axis)
        ends = count - 1
        head = lax.slice_in_dim(cells, 0, width, axis=dim)
        tail = lax.slice_in_dim(cells, cells.shape[dim] - width, cells.shape[dim], axis=dim)
        cells = jnp.concatenate(
            [
                lax.ppermute(tail, axis, [(i, (i + 1) % count) for i in range(ends)]),
                cells,
                lax.ppermute(head, axis, [((i + 1) % count, i) for i in range(ends)]),
            ],
            axis=dim,
        )
    return cells


def matmul_high(left_op, right_op):
    return jnp.dot(
        left_op, right_op, precision=lax.Precision.HIGHEST, preferred_element_type=jnp.float32
    )


def complex_product(left_re, left_im, right_re, right_im):
    return (
        matmul_high(left_re, right_re) - matmul_high(left_im, right_im),
        matmul_high(left_re, right_im) + matmul_high(left_im, right_re),
    )


def real_left(left_re, left_im, right_op):
    return (matmul_high(left_re, right_op), matmul_high(left_im, right_op))


def phase_gradient(phases, window, target, amplitude, cosine, sine_neg):
    extent = window.shape[0]
    win_size = phases.shape[0]
    core_size = target.shape[0]
    margin = (extent - core_size) // 2
    core_rows = slice(margin, margin + core_size)
    inverse_total = 1.0 / (extent * extent * jnp.sum(amplitude * amplitude))
    pupil_re = amplitude * jnp.cos(phases)
    pupil_im = amplitude * jnp.sin(phases)
    half_re, half_im = complex_product(
        cosine[:, :win_size], sine_neg[:, :win_size], pupil_re, pupil_im
    )
    far_re, far_im = complex_product(half_re, half_im, cosine[:win_size, :], sine_neg[:win_size, :])
    spread = (far_re * far_re + far_im * far_im) * inverse_total

    def spectrum(values):
        part_re, part_im = real_left(cosine, sine_neg, values)
        return complex_product(part_re, part_im, cosine, sine_neg)

    spread_re, spread_im = spectrum(spread)
    object_re, object_im = spectrum(window)
    prod_re = spread_re * object_re - spread_im * object_im
    prod_im = spread_re * object_im + spread_im * object_re
    rows_re, rows_im = complex_product(cosine[core_rows], -sine_neg[core_rows], prod_re, prod_im)
    model_image = (
        matmul_high(rows_re, cosine[:, core_rows]) + matmul_high(rows_im, sine_neg[:, core_rows])
    ) / (extent * extent)
    residual = (model_image - target) * (win_size * extent / core_size)
    grad_re, grad_im = real_left(cosine[:, core_rows], sine_neg[:, core_rows], residual)
    spec_re, spec_im = complex_product(
        grad_re, grad_im, cosine[core_rows, :], sine_neg[core_rows, :]
    )
    corr_re = spec_re * object_re + spec_im * object_im
    corr_im = spec_im * object_re - spec_re * object_im
    wave_re, wave_im = complex_product(cosine, -sine_neg, corr_re, corr_im)
    spread_grad = (matmul_high(wave_re, cosine) + matmul_high(wave_im, sine_neg)) / (
        extent * extent
    )
    back_re, back_im = complex_product(
        cosine[:win_size, :], -sine_neg[:win_size, :], far_re * spread_grad, far_im * spread_grad
    )
    out_re, out_im = complex_product(
        back_re, back_im, cosine[:, :win_size], -sine_neg[:, :win_size]
    )
    return 2.0 * inverse_total * (pupil_re * out_im - pupil_im * out_re)


def frame_total(values):
    return lax.psum_scatter(values, "frame", scatter_dimension=2, tiled=True)


def body(screens, row_offsets, col_offsets, amplitude, object_strip, observed):
    patch_count = lax.axis_size("patch")
    place = lax.axis_index("patch")
    frame_id = lax.axis_index("frame")
    layer_count, tile_rows, screen_cols = screens.shape
    win_size = amplitude.shape[0]
    extent = object_strip.shape[0]
    per_device = observed.shape[2] // CORE
    angle_index = jnp.arange(extent, dtype=jnp.int32)
    angles = (angle_index[:, None] * angle_index[None, :] % extent).astype(jnp.float32) * (
        2.0 * math.pi / extent
    )
    cosine = jnp.cos(angles)
    sine_neg = -jnp.sin(angles)
    patch_ids = (
        jnp.arange(patch_count, dtype=jnp.int32)[None, :] * per_device
        + jnp.arange(per_device, dtype=jnp.int32)[:, None]
    )
    rows_by = jnp.moveaxis(row_offsets[frame_id][:, patch_ids], 1, 0)
    cols_by = jnp.moveaxis(col_offsets[frame_id][:, patch_ids], 1, 0)
    my_rows = rows_by[:, :, place]
    extended = padded(object_strip, (("patch", 1),), HALO)
    windows = jnp.stack([extended])
    targets = observed[0].reshape(CORE, per_device, CORE).transpose(1, 0, 2)

    def cut_band(sheet, column):
        return lax.dynamic_slice_in_dim(sheet, column, win_size, 1)

    bands = jax.vmap(
        lambda member_cols: jax.vmap(
            lambda sheet, layer_cols: jax.vmap(lambda column: cut_band(sheet, column))(layer_cols)
        )(screens, member_cols)
    )(cols_by)
    received = lax.all_to_all(bands, "patch", split_axis=2, concat_axis=2, tiled=True)
    columns = received.reshape(per_device, layer_count, patch_count * tile_rows, win_size)

    def pick_rows(column_band, top_row):
        return lax.dynamic_slice_in_dim(column_band, top_row, win_size, 0)

    phases = jax.vmap(jax.vmap(pick_rows))(columns, my_rows).sum(axis=1)
    gradients = lax.map(
        lambda packed: phase_gradient(packed[0], packed[1], packed[2], amplitude, cosine, sine_neg),
        (phases, windows, targets),
    )

    def place_band(gradient, top_row):
        return lax.dynamic_update_slice_in_dim(
            jnp.zeros((patch_count * tile_rows, win_size), jnp.float32), gradient, top_row, 0
        )

    outgoing = jax.vmap(
        lambda gradient, member_rows: jax.vmap(lambda top_row: place_band(gradient, top_row))(
            member_rows
        )
    )(gradients, my_rows)
    returned = lax.all_to_all(
        outgoing.reshape(per_device, layer_count, patch_count, tile_rows, win_size),
        "patch",
        split_axis=2,
        concat_axis=2,
        tiled=True,
    )

    def add_band(source, running):
        for layer_id in range(layer_count):
            corner = (jnp.int32(layer_id), jnp.int32(0), cols_by[0, layer_id, source])
            current = lax.dynamic_slice(running, corner, (1, tile_rows, win_size))
            running = lax.dynamic_update_slice(
                running, current + returned[0, layer_id, source][None], corner
            )
        return running

    summed = lax.fori_loop(0, patch_count, add_band, jnp.zeros_like(screens))
    result = frame_total(summed)
    return result


def solution(mesh):
    in_specs = (P(None, "patch", None), P(), P(), P(), P(None, "patch"), P("frame", None, "patch"))
    out_specs = P(None, "patch", "frame")
    return jax.shard_map(body, mesh=mesh, in_specs=in_specs, out_specs=out_specs, check_vma=False)
```

profile of v0, /device:TPU:0, one launch (start us, length us, event | category | flops | bytes accessed | tf_op | source)
XLA Modules:
  0.0 294.9 jit_solution(6073187552833694168)
XLA Ops:
  8.1 6.2 %copy.38 = f32[2,64,4096]{1,0,2:T(2,128)} copy(f32[2,64,4096]{2,1,0:T(8,128)} %param.8) | data formatting | bytes 4194304 | tf_op args[0]
  14.2 4.2 %gather_fusion.2 = f32[16,64,256]{1,0,2:T(8,128)S(1)} fusion(f32[2,64,4096]{1,0,2:T(2,128)} %copy.38, s32[16]{0:T(128)S(1)} %reshape.144), kind=kCustom, calls=%fused_computation.2 | custom fusion | bytes 2097344 | tf_op jit(solution)/shard_map/vmap(vmap(vmap()))/gather | solution.py:123
  18.5 2.0 copy.39
  20.5 7.4 %all-to-all-start = ((f32[1,2,8,64,256]{4,3,1,0,2:T(8,128)}), f32[1,2,8,64,256]{4,3,1,0,2:T(8,128)S(1)}, u32[]{:S(2)}, u32[]{:S(2)}) async-start(f32[1,2,8,64,256]{4,3,1,0,2:T(8,128)} %copy.39), calls=%async_computation | async-start | bytes 2097152 | tf_op jit(solution)/shard_map/all_to_all | solution.py:130
  28.0 4.6 %collective-permute-start = (f32[384,64]{1,0:T(8,128)S(1)}, f32[384,64]{1,0:T(8,128)}, u32[]{:S(2)}, u32[]{:S(2)}) collective-permute-start(f32[384,64]{1,0:T(8,128)S(1)} %get-tuple-element.151), channel_id=1, source_target_pairs={{0,4},{4,8},{8,12},{12,16},{16,20},{20,24},{24,28},{1,5},{5,9},{9,... | collective-permute-start | bytes 294920 | tf_op jit(solution)/shard_map/ppermute | solution.py:20
  32.6 1.8 collective-permute-start.1
  36.9 2.2 fusion.13
  39.1 2.3 fusion.16
  41.5 2.5 collective-permute-done
  44.1 4.7 %fusion.68 = f32[384,384]{1,0:T(8,128)S(1)} fusion(f32[384,64]{1,0:T(8,128)} %collective-permute-done.1, f32[384,256]{1,0:T(8,128)S(1)} %copy-done.4, f32[384,64]{1,0:T(8,128)} %collective-permute-done), kind=kOutput, calls=%fused_computation.105 | convolution fusion | flops 681099264 | bytes 1179648 | tf_op jit(solution)/shard_map/while/body/eval_jaxpr/dot_general | solution.py:30
  48.8 4.9 %fusion.67 = f32[384,384]{1,0:T(8,128)S(1)} fusion(f32[384,64]{1,0:T(8,128)} %collective-permute-done.1, f32[384,256]{1,0:T(8,128)S(1)} %copy-done.4, f32[384,64]{1,0:T(8,128)} %collective-permute-done), kind=kOutput, calls=%fused_computation.104 | convolution fusion | flops 681246720 | bytes 1179648 | tf_op jit(solution)/shard_map/while/body/eval_jaxpr/dot_general | solution.py:30
  53.7 3.5 %fusion.91 = f32[384,384]{1,0:T(8,128)S(1)} fusion(f32[384,384]{1,0:T(8,128)S(1)} %fusion.68), kind=kOutput, calls=%fused_computation.116 | convolution fusion | flops 680951808 | bytes 1179648 | tf_op jit(solution)/shard_map/while/body/eval_jaxpr/dot_general | solution.py:30
  57.2 3.5 %fusion.83 = f32[384,384]{1,0:T(8,128)S(1)} fusion(f32[384,384]{1,0:T(8,128)S(1)} %fusion.68), kind=kOutput, calls=%fused_computation.113 | convolution fusion | flops 680804352 | bytes 1179648 | tf_op jit(solution)/shard_map/while/body/eval_jaxpr/dot_general | solution.py:30
  60.7 4.9 %convolution_add_fusion.2 = f32[384,384]{1,0:T(8,128)} fusion(f32[384,384]{1,0:T(8,128)S(1)} %fusion.91, f32[384,384]{1,0:T(8,128)S(1)} %fusion.67), kind=kOutput, calls=%fused_computation.14 | convolution fusion | flops 680951808 | bytes 1769472 | tf_op jit(solution)/shard_map/while/body/eval_jaxpr/dot_general | solution.py:30
  65.6 5.0 %convolution_subtract_fusion.1 = f32[384,384]{1,0:T(8,128)} fusion(f32[384,384]{1,0:T(8,128)S(1)} %fusion.83, f32[384,384]{1,0:T(8,128)S(1)} %fusion.67), kind=kOutput, calls=%fused_computation.16 | convolution fusion | flops 681099264 | bytes 1769472 | tf_op jit(solution)/shard_map/while/body/eval_jaxpr/dot_general | solution.py:30
  71.4 2.6 gather_fusion.3
  74.7 1.3 fusion.58
  76.0 1.3 fusion.56
  77.3 1.3 convolution_subtract_fusion.5
  80.3 1.3 convolution_add_fusion.6
  83.2 4.0 %fusion.98 = f32[384,384]{1,0:T(8,128)S(1)} fusion(f32[384,384]{1,0:T(8,128)S(1)} %convolution_add_fusion.5, f32[384,384]{1,0:T(8,128)S(1)} %convolution_subtract_fusion.4, f32[]{:T(128)S(6)} %div.12), kind=kOutput, calls=%fused_computation.118 | convolution fusion | flops 681541632 | bytes 1769476 | tf_op jit(solution)/shard_map/while/body/eval_jaxpr/dot_general | solution.py:30
  87.2 3.6 %fusion.88 = f32[384,384]{1,0:T(8,128)S(1)} fusion(f32[384,384]{1,0:T(8,128)S(1)} %convolution_add_fusion.5, f32[384,384]{1,0:T(8,128)S(1)} %convolution_subtract_fusion.4, f32[]{:T(128)S(6)} %div.12), kind=kOutput, calls=%fused_computation.115 | convolution fusion | flops 681394176 | bytes 1769476 | tf_op jit(solution)/shard_map/while/body/eval_jaxpr/dot_general | solution.py:30
  90.8 3.5 %fusion.86 = f32[384,384]{1,0:T(8,128)S(1)} fusion(f32[384,384]{1,0:T(8,128)S(1)} %fusion.88), kind=kOutput, calls=%fused_computation.114 | convolution fusion | flops 680804352 | bytes 1179648 | tf_op jit(solution)/shard_map/while/body/eval_jaxpr/dot_general | solution.py:30
  94.3 3.7 %fusion.93 = f32[384,384]{1,0:T(8,128)S(1)} fusion(f32[384,384]{1,0:T(8,128)S(1)} %fusion.88), kind=kOutput, calls=%fused_computation.117 | convolution fusion | flops 680951808 | bytes 1179648 | tf_op jit(solution)/shard_map/while/body/eval_jaxpr/dot_general | solution.py:30
  98.0 3.5 %convolution_subtract_fusion.2 = f32[384,384]{1,0:T(8,128)S(1)} fusion(f32[384,384]{1,0:T(8,128)S(1)} %fusion.86, f32[384,384]{1,0:T(8,128)S(1)} %fusion.98), kind=kOutput, calls=%fused_computation.17 | convolution fusion | flops 681099264 | bytes 1769472 | tf_op jit(solution)/shard_map/while/body/eval_jaxpr/dot_general | solution.py:30
  101.5 3.5 %multiply_add_fusion.1 = (f32[384,384]{1,0:T(8,128)S(1)}, f32[384,384]{1,0:T(8,128)S(1)}) fusion(f32[384,384]{1,0:T(8,128)S(1)} %copy-done.3, f32[384,384]{1,0:T(8,128)S(1)} %convolution_subtract_fusion.2, f32[384,384]{1,0:T(8,128)S(1)} %copy-done.2, f32[384,384]{1,0:T(8,128)S(1)} %fusion.93, f32[384,384]{1,0:T(8,128)S(1)} %fusion.98), kind=kOutput, calls=%fused_computation.45 | convolution fusion | flops 681836544 | bytes 4128768 | tf_op jit(solution)/shard_map/while/body/eval_jaxpr/dot_general | solution.py:30
  106.9 1.2 convolution_add_fusion.8
  114.7 4.1 %fusion.75 = f32[384,384]{1,0:T(8,128)S(1)} fusion(f32[384,384]{1,0:T(8,128)S(1)} %get-tuple-element.147), kind=kOutput, calls=%fused_computation.110 | convolution fusion | flops 680804352 | bytes 1179648 | tf_op jit(solution)/shard_map/while/body/eval_jaxpr/dot_general | solution.py:30
  118.9 4.1 %fusion.79 = f32[384,384]{1,0:T(8,128)S(1)} fusion(f32[384,384]{1,0:T(8,128)S(1)} %get-tuple-element.148), kind=kOutput, calls=%fused_computation.112 | convolution fusion | flops 680804352 | bytes 1179648 | tf_op jit(solution)/shard_map/while/body/eval_jaxpr/dot_general | solution.py:30
  123.0 4.1 %convolution_add_fusion.1 = f32[384,384]{1,0:T(8,128)S(1)} fusion(f32[384,384]{1,0:T(8,128)S(1)} %fusion.75, f32[384,384]{1,0:T(8,128)S(1)} %get-tuple-element.148), kind=kOutput, calls=%fused_computation.12 | convolution fusion | flops 680951808 | bytes 1769472 | tf_op jit(solution)/shard_map/while/body/eval_jaxpr/dot_general | solution.py:30
  127.1 4.5 %convolution_subtract_fusion = f32[384,384]{1,0:T(8,128)S(1)} fusion(f32[384,384]{1,0:T(8,128)S(1)} %fusion.79, f32[384,384]{1,0:T(8,128)S(1)} %get-tuple-element.147), kind=kOutput, calls=%fused_computation.13 | convolution fusion | flops 680951808 | bytes 1769472 | tf_op jit(solution)/shard_map/while/body/eval_jaxpr/dot_general | solution.py:30
  131.6 3.5 %fusion.77 = f32[384,384]{1,0:T(8,128)S(1)} fusion(f32[384,384]{1,0:T(8,128)S(1)} %convolution_subtract_fusion), kind=kOutput, calls=%fused_computation.111 | convolution fusion | flops 680804352 | bytes 1179648 | tf_op jit(solution)/shard_map/while/body/eval_jaxpr/dot_general | solution.py:30
  135.1 3.5 %fusion = f32[384,384]{1,0:T(8,128)S(1)} fusion(f32[384,384]{1,0:T(8,128)S(1)} %fusion.77, f32[384,384]{1,0:T(8,128)S(1)} %convolution_add_fusion.1), kind=kOutput, calls=%fused_computation.18 | convolution fusion | flops 681246720 | bytes 1769472 | tf_op jit(solution)/shard_map/while/body/eval_jaxpr/dot_general | solution.py:30
  142.6 1.1 convolution_add_fusion.7
  143.7 1.3 fusion.2
  145.1 1.4 fusion.5
  146.6 17.1 %while.19 = (s32[]{:T(128)}, f32[1,2,512,256]{3,2,1,0:T(8,128)S(1)}, s32[2,4]{1,0:T(2,128)S(1)}, f32[2,256,256]{2,1,0:T(8,128)S(1)}, s32[]{:T(128)}, /*index=5*/s32[4]{0:T(128)S(1)}, s32[]{:T(128)}) while((s32[]{:T(128)}, f32[1,2,512,256]{3,2,1,0:T(8,128)S(1)}, s32[2,4]{1,0:T(2,128)S(1)}, f32[2,256,256]{2,1,0:T(8,128)S(1)}, s32[]{:T(128)}, ...), condition=%wide.while_cond, body=%wide.while_body.sunk | while | flops 65565 | bytes 1310915 | solution.py:143
  147.2 3.2 %and_reduce_fusion.2 = pred[]{:T(512)} fusion(s32[4]{0:T(128)S(1)} %get-tuple-element.240, s32[1]{0:T(128)} %bitcast.89, s32[1]{0:T(128)} %bitcast.90, s32[1]{0:T(128)} %bitcast.91, s32[1]{0:T(128)} %bitcast.92), kind=kLoop, calls=%fused_computation.9.clone.1 | loop fusion | flops 27 | bytes 33 | tf_op jit(solution)/shard_map/vmap(vmap(vmap()))/scatter
  150.4 1.9 bitcast_select_fusion.2
  152.3 3.1 %dynamic-update-slice.3 = f32[1,2,512,256]{3,2,1,0:T(8,128)S(1)} dynamic-update-slice(f32[1,2,512,256]{3,2,1,0:T(8,128)S(1)} %get-tuple-element.229, f32[1,1,256,256]{3,2,1,0:T(8,128)S(1)} %bitcast_select_fusion.2, s32[]{:T(128)} %constant.89.clone.1..sunk.1, s32[]{:T(128)} %bitcast.87, s32[]{:T(128)} %bitcast.88, s32[]{:T(128)} %constant.89.clone.1..sunk.1) | dynamic-update-slice | bytes 524292 | tf_op jit(solution)/shard_map/vmap(vmap(vmap()))/scatter
  156.1 3.2 %and_reduce_fusion.2 = pred[]{:T(512)} fusion(s32[4]{0:T(128)S(1)} %get-tuple-element.240, s32[1]{0:T(128)} %bitcast.89, s32[1]{0:T(128)} %bitcast.90, s32[1]{0:T(128)} %bitcast.91, s32[1]{0:T(128)} %bitcast.92), kind=kLoop, calls=%fused_computation.9.clone.1 | loop fusion | flops 27 | bytes 33 | tf_op jit(solution)/shard_map/vmap(vmap(vmap()))/scatter
  159.2 1.9 bitcast_select_fusion.2
  161.1 2.6 dynamic-update-slice.3
  164.8 16.4 %all-to-all-start.1 = ((f32[1,2,8,64,256]{4,3,1,0,2:T(8,128)}), f32[1,2,8,64,256]{4,3,1,0,2:T(8,128)S(1)}, u32[]{:S(2)}, u32[]{:S(2)}) async-start(f32[1,2,8,64,256]{4,3,1,0,2:T(8,128)} %copy.42), calls=%async_computation.1 | async-start | bytes 2097152 | tf_op jit(solution)/shard_map/all_to_all | solution.py:152
  181.2 25.7 %all-to-all-done.1 = f32[1,2,8,64,256]{4,3,1,0,2:T(8,128)S(1)} async-done(((f32[1,2,8,64,256]{4,3,1,0,2:T(8,128)}), f32[1,2,8,64,256]{4,3,1,0,2:T(8,128)S(1)}, u32[]{:S(2)}, u32[]{:S(2)}) %all-to-all-start.1) | async-done | bytes 1048608 | tf_op jit(solution)/shard_map/all_to_all | solution.py:152
  207.2 48.4 %while.18 = (s32[]{:T(128)}, f32[2,64,4096]{2,1,0:T(8,128)S(1)}, s32[1,2,8]{2,1,0:T(2,128)S(1)}, f32[1,2,8,64,256]{4,3,2,1,0:T(8,128)S(1)}, s32[]{:T(128)}, /*index=5*/s32[]{:T(128)}, s32[]{:T(128)}) while((s32[]{:T(128)}, f32[2,64,4096]{2,1,0:T(8,128)S(1)}, s32[1,2,8]{2,1,0:T(2,128)S(1)}, f32[1,2,8,64,256]{4,3,2,1,0:T(8,128)S(1)}, s32[]{:T(128)}, ...), condition=%wide.region_4.5_spmd, body=%wide.region_3.4_spmd.sunk | while | flops 32776 | bytes 655549 | solution.py:169
  255.7 1.3 copy-done.1
  257.0 30.9 %reduce-scatter.2.cloned.1.call-done = f32[2,64,1024]{2,1,0:T(8,128)} async-done(((f32[2,64,4096]{2,1,0:T(8,128)}), f32[2,64,1024]{2,1,0:T(8,128)}) %reduce-scatter.2.cloned.1.call-update) | async-done | bytes 524304 | tf_op jit(solution)/shard_map/reduce_scatter | solution.py:94
  (113 shorter events, 42.8 us)
Async XLA Ops:
  20.5 7.4 %copy-start.4 = (f32[384,256]{1,0:T(8,128)S(1)}, f32[384,256]{1,0:T(8,128)}, u32[]{:S(2)}) copy-start(f32[384,256]{1,0:T(8,128)} %param.12) | copy-start | bytes 1179652
  20.5 14.6 %copy-start.7 = (s32[2]{0:T(128)S(1)}, s32[2]{0:T(128)}, u32[]{:S(2)}) copy-start(s32[2]{0:T(128)} %constant.97.clone.1) | copy-start | bytes 28
  20.5 14.9 %copy-start = (f32[256,256]{1,0:T(8,128)S(1)}, f32[256,256]{1,0:T(8,128)}, u32[]{:S(2)}) copy-start(f32[256,256]{1,0:T(8,128)} %param.11) | copy-start | bytes 786436
  20.5 50.1 %all-to-all-start = ((f32[1,2,8,64,256]{4,3,1,0,2:T(8,128)}), f32[1,2,8,64,256]{4,3,1,0,2:T(8,128)S(1)}, u32[]{:S(2)}, u32[]{:S(2)}) async-start(f32[1,2,8,64,256]{4,3,1,0,2:T(8,128)} %copy.39), calls=%async_computation | async-start | bytes 2097152 | tf_op jit(solution)/shard_map/all_to_all | solution.py:130
  28.0 16.0 %collective-permute-start = (f32[384,64]{1,0:T(8,128)S(1)}, f32[384,64]{1,0:T(8,128)}, u32[]{:S(2)}, u32[]{:S(2)}) collective-permute-start(f32[384,64]{1,0:T(8,128)S(1)} %get-tuple-element.151), channel_id=1, source_target_pairs={{0,4},{4,8},{8,12},{12,16},{16,20},{20,24},{24,28},{1,5},{5,9},{9,... | collective-permute-start | bytes 294920 | tf_op jit(solution)/shard_map/ppermute | solution.py:20
  32.6 11.5 %collective-permute-start.1 = (f32[384,64]{1,0:T(8,128)S(1)}, f32[384,64]{1,0:T(8,128)}, u32[]{:S(2)}, u32[]{:S(2)}) collective-permute-start(f32[384,64]{1,0:T(8,128)S(1)} %get-tuple-element.152), channel_id=1, source_target_pairs={{4,0},{8,4},{12,8},{16,12},{20,16},{24,20},{28,24},{5,1},{9,5},{13... | collective-permute-start | bytes 294920 | tf_op jit(solution)/shard_map/ppermute | solution.py:22
  94.3 7.2 %copy-start.2 = (f32[384,384]{1,0:T(8,128)S(1)}, f32[384,384]{1,0:T(8,128)}, u32[]{:S(2)}) copy-start(f32[384,384]{1,0:T(8,128)} %convolution_add_fusion.2) | copy-start | bytes 1769476
  94.3 7.2 %copy-start.3 = (f32[384,384]{1,0:T(8,128)S(1)}, f32[384,384]{1,0:T(8,128)}, u32[]{:S(2)}) copy-start(f32[384,384]{1,0:T(8,128)} %convolution_subtract_fusion.1) | copy-start | bytes 1769476
  106.8 2.8 copy-start.5
  145.0 1.5 copy-start.6
  164.8 42.1 %all-to-all-start.1 = ((f32[1,2,8,64,256]{4,3,1,0,2:T(8,128)}), f32[1,2,8,64,256]{4,3,1,0,2:T(8,128)S(1)}, u32[]{:S(2)}, u32[]{:S(2)}) async-start(f32[1,2,8,64,256]{4,3,1,0,2:T(8,128)} %copy.42), calls=%async_computation.1 | async-start | bytes 2097152 | tf_op jit(solution)/shard_map/all_to_all | solution.py:152
  181.1 106.8 %reduce-scatter.2.cloned.1.call-start = ((), (), s32[]{:S(2)}) async-start(), calls=%async_computation.3 | async-start | bytes 2621440 | tf_op jit(solution)/shard_map/reduce_scatter | solution.py:94
  255.6 1.3 copy-start.1
Sparse Core Ops, SparseCore 0:
  257.1 30.7 reduce-scatter.1
where the time goes:
time: 299 us; the launch traced here: 295 us
  matrix products  97.9 us (33%)
  waiting for transfers between devices  59.2 us (20%)
  local copies, waits for them, and re-layouts  45.8 us (15%)
  starting transfers between devices  30.2 us (10%)
  loops' own time  29.2 us (10%)
  other arithmetic  17.7 us (6%)
  between operations  14.9 us (5%)
    dot_general x46, matrix products, matmul_high(): jnp.dot(left_op, right_op, precision=lax.Precision.HIGHEST, preferred_ele...  97.9 us
    reduce_scatter x1, waiting for transfers between devices, frame_total(): return lax.psum_scatter(values, 'frame', scatter_dimension=2, tiled=True)  30.9 us
    another operation x1, loops' own time, body(): summed = lax.fori_loop(0, patch_count, add_band, jnp.zeros_like(screens))  29.1 us
    all_to_all x1, waiting for transfers between devices, body(): lax.all_to_all(outgoing.reshape(per_device, layer_count, patch_count, til...  25.7 us
    all_to_all x1, starting transfers between devices, body(): lax.all_to_all(outgoing.reshape(per_device, layer_count, patch_count, til...  16.4 us
    dynamic_update_slice x16, local copies, waits for them, and re-layouts, add_band(): lax.dynamic_update_slice(running, current + returned[0, layer_id, source]...  12.9 us
    scatter x4, other arithmetic  10.1 us
    unnamed x20, local copies, waits for them, and re-layouts  7.52 us
  transfers between devices with their start and end apart: 5, of which 4 were waited for; matrix products, arithmetic and copies ran while one was open for 11% of the time, Pallas kernels for 0%

commit v1 on v0

v1 whole, which is shorter than its diff:
```python
import functools

import jax
import jax.numpy as jnp
import numpy as np
from jax import lax
from jax.experimental import pallas as pl
from jax.experimental.pallas import tpu as pltpu
from jax.sharding import PartitionSpec as P

CORE = 256
HALO = 64
LANES = 128
SUBLANES = 8
RADIX = 3
HALF_ROOT3 = float(np.sqrt(3.0) / 2)
VMEM_LIMIT = 48 * 1024 * 1024
VMEM_SPEC = pl.BlockSpec(memory_space=pltpu.VMEM)
SMEM_SPEC = pl.BlockSpec(memory_space=pltpu.SMEM)


def split(values):
    high = values.astype(jnp.bfloat16)
    return high, (values - high.astype(jnp.float32)).astype(jnp.bfloat16)


def product(left, right):
    dot = functools.partial(jnp.dot, preferred_element_type=jnp.float32)
    return dot(left[0], right[1]) + dot(left[1], right[0]) + dot(left[0], right[0])


def left_product(matrix, values):
    return product(matrix, split(values))


def right_product(values, matrix):
    return product(split(values), matrix)


def transform_matrices(extent):
    part = extent // RADIX
    index = np.arange(part)
    angles = (pow(RADIX, -1, part) * index[:, None] * index[None, :] % part) * (2 * np.pi / part)
    cosine, sine = np.cos(angles), np.sin(angles)
    forward = np.block([[cosine, sine], [-sine, cosine]]).astype(np.float32)
    arrays = []
    for matrix in (forward, forward.T):
        high = matrix.astype(jnp.bfloat16)
        low = (matrix - high.astype(np.float32)).astype(jnp.bfloat16)
        arrays += [high, low]
    return arrays


def residue(shape, axis):
    return lax.broadcasted_iota(jnp.int32, shape, axis) % RADIX


def pick(blocks, which):
    result = blocks[0]
    for number in range(1, RADIX):
        result = jnp.where(which == number, blocks[number], result)
    return result


def to_residues(blocks, axis):
    like = blocks[0]
    blocks = list(blocks) + [jnp.zeros_like(like)] * (RADIX - len(blocks))
    rest = residue(like.shape, axis)
    part = like.shape[axis]
    inverse = pow(part, -1, RADIX)
    return [pick(blocks, (inverse * (j + 2 * rest)) % RADIX) for j in range(RADIX)]


def to_natural(blocks, axis, count):
    rest = residue(blocks[0].shape, axis)
    part = blocks[0].shape[axis]
    return [pick(blocks, (part * j + rest) % RADIX) for j in range(count)]


def blocks_of(values, axis):
    count = values.shape[axis] // LANES
    return [lax.slice_in_dim(values, j * LANES, (j + 1) * LANES, axis=axis) for j in range(count)]


def butterfly(re, im, sign):
    sum_re, sum_im = re[1] + re[2], im[1] + im[2]
    mid_re, mid_im = re[0] - 0.5 * sum_re, im[0] - 0.5 * sum_im
    turn_re = (sign * HALF_ROOT3) * (re[1] - re[2])
    turn_im = (sign * HALF_ROOT3) * (im[1] - im[2])
    return (
        [re[0] + sum_re, mid_re - turn_im, mid_re + turn_im],
        [im[0] + sum_im, mid_im + turn_re, mid_im - turn_re],
    )


def halves(values, axis):
    size = values.shape[axis] // 2
    return (
        lax.slice_in_dim(values, 0, size, axis=axis),
        lax.slice_in_dim(values, size, 2 * size, axis=axis),
    )


def columns_forward(re, im, turned):
    re, im = butterfly(re, im, 1.0)
    pairs = [
        halves(right_product(jnp.concatenate([a, b], axis=1), turned), 1) for a, b in zip(re, im)
    ]
    return jnp.concatenate([p[0] for p in pairs], axis=1), jnp.concatenate(
        [p[1] for p in pairs], axis=1
    )


def columns_inverse(re, im, plain):
    pairs = [
        halves(right_product(jnp.concatenate([a, b], axis=1), plain), 1)
        for a, b in zip(blocks_of(re, 1), blocks_of(im, 1))
    ]
    return butterfly([p[0] for p in pairs], [p[1] for p in pairs], -1.0)


def rows_forward(re, im, plain):
    re, im = butterfly(re, im, 1.0)
    pairs = [
        halves(left_product(plain, jnp.concatenate([a, b], axis=0)), 0) for a, b in zip(re, im)
    ]
    return jnp.concatenate([p[0] for p in pairs], axis=0), jnp.concatenate(
        [p[1] for p in pairs], axis=0
    )


def rows_inverse(re, im, turned):
    pairs = [
        halves(left_product(turned, jnp.concatenate([a, b], axis=0)), 0)
        for a, b in zip(blocks_of(re, 0), blocks_of(im, 0))
    ]
    return butterfly([p[0] for p in pairs], [p[1] for p in pairs], -1.0)


def rows_forward_real(blocks, plain):
    part = blocks[0].shape[0]
    total = blocks[1] + blocks[2]
    narrow = (plain[0][:, :part], plain[1][:, :part])
    first = halves(left_product(narrow, blocks[0] + total), 0)
    turned = jnp.concatenate(
        [blocks[0] - 0.5 * total, HALF_ROOT3 * (blocks[1] - blocks[2])], axis=0
    )
    second = halves(left_product(plain, turned), 0)
    return jnp.concatenate([first[0], second[0]], axis=0), jnp.concatenate(
        [first[1], second[1]], axis=0
    )


def rows_inverse_real(re, im, turned):
    re, im = blocks_of(re, 0), blocks_of(im, 0)
    part = re[0].shape[0]
    short = (turned[0][:part], turned[1][:part])
    base = left_product(short, jnp.concatenate([re[0], im[0]], axis=0))
    pair_re, pair_im = halves(left_product(turned, jnp.concatenate([re[1], im[1]], axis=0)), 0)
    near, far = base - pair_re, (2 * HALF_ROOT3) * pair_im
    return [base + 2.0 * pair_re, near + far, near - far]


def sine_cosine(angle):
    quarter = jnp.floor(angle * np.float32(2 / np.pi) + 0.5)
    rest = angle - quarter * np.float32(1.5703125)
    rest = rest - quarter * np.float32(4.837512969970703125e-4)
    rest = rest - quarter * np.float32(7.549789948768648e-8)
    square = rest * rest
    sine = rest + rest * square * (
        -1.6666654611e-1 + square * (8.3321608736e-3 - 1.9515295891e-4 * square)
    )
    cosine = (
        1.0
        - 0.5 * square
        + square
        * square
        * (4.166664568298827e-2 + square * (-1.388731625493765e-3 + 2.443315711809948e-5 * square))
    )
    turn = quarter.astype(jnp.int32) & 3
    swap = (turn & 1) == 1
    out_sine = jnp.where(swap, cosine, sine)
    out_cosine = jnp.where(swap, sine, cosine)
    out_sine = jnp.where(turn >= 2, -out_sine, out_sine)
    out_cosine = jnp.where((turn == 1) | (turn == 2), -out_cosine, out_cosine)
    return out_sine, out_cosine


def object_kernel(window_ref, fh, fl, th, tl, re_ref, im_ref):
    plain, turned = (fh[...], fl[...]), (th[...], tl[...])
    extent = window_ref.shape[0]
    values = window_ref[...] * (1.0 / (extent * extent))
    re, im = rows_forward_real(to_residues(blocks_of(values, 0), 0), plain)
    re, im = columns_forward(
        to_residues(blocks_of(re, 1), 1), to_residues(blocks_of(im, 1), 1), turned
    )
    re_ref[...] = re
    im_ref[...] = im


def pair_gradient(phases, target, amplitude, object_re, object_im, plain, turned):
    win_size = phases.shape[0]
    extent = object_re.shape[1]
    naturals = win_size // LANES
    inverse_total = 1.0 / (extent * extent * jnp.sum(amplitude * amplitude))
    sine, cosine = sine_cosine(phases)
    pupil_re, pupil_im = amplitude * cosine, amplitude * sine

    def parts(values, axis):
        return to_residues(blocks_of(values, axis), axis)

    re, im = rows_forward(parts(pupil_re, 0), parts(pupil_im, 0), plain)
    far_re, far_im = columns_forward(parts(re, 1), parts(im, 1), turned)
    spread = (far_re * far_re + far_im * far_im) * inverse_total
    re, im = rows_forward_real(blocks_of(spread, 0), plain)
    re, im = columns_forward(blocks_of(re, 1), blocks_of(im, 1), turned)
    re, im = re * object_re - im * object_im, re * object_im + im * object_re
    re, im = columns_inverse(re, im, plain)
    re = jnp.concatenate(to_natural(re, 1, naturals), axis=1)
    im = jnp.concatenate(to_natural(im, 1, naturals), axis=1)
    model = jnp.concatenate(to_natural(rows_inverse_real(re, im, turned), 0, naturals), axis=0)
    residual = (model - target) * (win_size * extent / target.shape[0])
    re, im = rows_forward_real(parts(residual, 0), plain)
    re, im = columns_forward(parts(re, 1), parts(im, 1), turned)
    re, im = re * object_re + im * object_im, im * object_re - re * object_im
    re, im = columns_inverse(re, im, plain)
    spread_grad = jnp.concatenate(
        rows_inverse_real(jnp.concatenate(re, axis=1), jnp.concatenate(im, axis=1), turned), axis=0
    )
    re, im = columns_inverse(far_re * spread_grad, far_im * spread_grad, plain)
    re = jnp.concatenate(to_natural(re, 1, naturals), axis=1)
    im = jnp.concatenate(to_natural(im, 1, naturals), axis=1)
    re, im = rows_inverse(re, im, turned)
    back_re = jnp.concatenate(to_natural(re, 0, naturals), axis=0)
    back_im = jnp.concatenate(to_natural(im, 0, naturals), axis=0)
    return 2.0 * inverse_total * (pupil_re * back_im - pupil_im * back_re)


def aligned(offset, unit, size, width):
    begin = jnp.minimum((offset // unit) * unit, size - width)
    return pl.multiple_of(begin, unit), offset - begin


def patch_kernel(
    rows_ref, bands_ref, target_ref, amplitude_ref, ore_ref, oim_ref, fh, fl, th, tl, out_ref, sheet
):
    count, layers, tile, win_size = bands_ref.shape
    reach = win_size + SUBLANES
    plain, turned = (fh[...], fl[...]), (th[...], tl[...])
    phases = None
    corners = []
    for layer in range(layers):
        for holder in range(count):
            sheet[layer, pl.ds(holder * tile, tile), :] = bands_ref[holder, layer]
        begin, shift = aligned(rows_ref[layer], SUBLANES, count * tile, reach)
        corners.append((begin, shift))
        rows = sheet[layer, pl.ds(begin, reach), :]
        rows = pltpu.roll(rows, jnp.where(shift == 0, 0, reach - shift), 0)[:win_size]
        phases = rows if phases is None else phases + rows
    gradient = pair_gradient(
        phases, target_ref[...], amplitude_ref[...], ore_ref[...], oim_ref[...], plain, turned
    )
    padded = jnp.concatenate([gradient, jnp.zeros((SUBLANES, win_size), jnp.float32)], axis=0)
    for layer in range(layers):
        begin, shift = corners[layer]
        sheet[layer] = jnp.zeros((count * tile, win_size), jnp.float32)
        sheet[layer, pl.ds(begin, reach), :] = pltpu.roll(padded, shift, 0)
        for holder in range(count):
            out_ref[holder, layer] = sheet[layer, pl.ds(holder * tile, tile), :]


def cut_kernel(cols_ref, screens_ref, out_ref):
    layers, tile, screen_cols = screens_ref.shape
    count, _, _, win_size = out_ref.shape
    reach = win_size + LANES

    @pl.loop(0, count)
    def _(patch):
        for layer in range(layers):
            begin, shift = aligned(cols_ref[layer, patch], LANES, screen_cols, reach)
            cells = screens_ref[layer, :, pl.ds(begin, reach)]
            cells = pltpu.roll(cells, jnp.where(shift == 0, 0, reach - shift), 1)
            out_ref[patch, layer] = cells[:, :win_size]


def add_kernel(cols_ref, frame_ref, bands_ref, keep_ref, send_ref, sheet):
    count, layers, tile, win_size = bands_ref.shape
    screen_cols = sheet.shape[2]
    reach = win_size + LANES
    chunks, _, _, width = keep_ref.shape
    sheet[...] = jnp.zeros_like(sheet)

    @pl.loop(0, count)
    def _(patch):
        for layer in range(layers):
            begin, shift = aligned(cols_ref[layer, patch], LANES, screen_cols, reach)
            cells = jnp.concatenate(
                [bands_ref[patch, layer], jnp.zeros((tile, LANES), jnp.float32)], axis=1
            )
            sheet[layer, :, pl.ds(begin, reach)] += pltpu.roll(cells, shift, 1)

    bit = frame_ref[0] & 1
    for chunk in range(chunks):
        for ref, low in ((keep_ref, bit), (send_ref, 1 - bit)):
            begin = pl.multiple_of((2 * chunk + low) * width, LANES)
            for layer in range(layers):
                ref[chunk, layer] = sheet[layer, :, pl.ds(begin, width)]


def call(kernel, out_shape, specs, scratch=(), flops=0, moved=0):
    return pl.pallas_call(
        kernel,
        out_shape=out_shape,
        in_specs=specs,
        out_specs=jax.tree.map(lambda _: VMEM_SPEC, out_shape),
        scratch_shapes=list(scratch),
        cost_estimate=pl.CostEstimate(flops=flops, bytes_accessed=moved, transcendentals=0),
        compiler_params=pltpu.CompilerParams(vmem_limit_bytes=VMEM_LIMIT),
    )


def frame_total(keep, send, frame_id):
    count = lax.axis_size("frame")
    step = 1
    while True:
        received = lax.ppermute(send, "frame", [(i, i ^ step) for i in range(count)])
        total = keep + received
        if total.shape[0] == 1:
            return total[0]
        step *= 2
        bit = (frame_id // step) % 2
        pairs = total.reshape((total.shape[0] // 2, 2) + total.shape[1:])
        keep = lax.dynamic_index_in_dim(pairs, bit, 1, keepdims=False)
        send = lax.dynamic_index_in_dim(pairs, 1 - bit, 1, keepdims=False)


def body(screens, row_offsets, col_offsets, amplitude, object_strip, observed):
    patch_count = lax.axis_size("patch")
    frame_count = lax.axis_size("frame")
    place = lax.axis_index("patch")
    frame_id = lax.axis_index("frame")
    layers, tile, screen_cols = screens.shape
    win_size = amplitude.shape[0]
    extent = object_strip.shape[0]
    width = screen_cols // frame_count
    float_of = lambda *shape: jax.ShapeDtypeStruct(shape, jnp.float32)
    matrices = [jnp.asarray(m) for m in transform_matrices(extent)]
    cols = lax.dynamic_index_in_dim(col_offsets, frame_id, 0, keepdims=False)
    rows = lax.dynamic_slice(row_offsets, (frame_id, 0, place), (1, layers, 1)).reshape(layers)

    bands = call(
        cut_kernel,
        float_of(patch_count, layers, tile, win_size),
        [SMEM_SPEC, VMEM_SPEC],
        moved=2 * screens.size * 4,
    )(cols, screens)
    received = lax.all_to_all(bands, "patch", split_axis=0, concat_axis=0, tiled=True)

    ends = patch_count - 1
    head = lax.slice_in_dim(object_strip, 0, HALO, axis=1)
    tail = lax.slice_in_dim(object_strip, object_strip.shape[1] - HALO, None, axis=1)
    right = lax.ppermute(head, "patch", [(i + 1, i) for i in range(ends)])
    left = lax.ppermute(tail, "patch", [(i, i + 1) for i in range(ends)])
    window = jnp.concatenate([object_strip, right, left], axis=1)
    window = jnp.concatenate([window[HALO:], window[:HALO]], axis=0)
    spectrum = float_of(2 * (extent // RADIX), extent)
    object_re, object_im = call(
        object_kernel, (spectrum, spectrum), [VMEM_SPEC] * 5, flops=3 * 10**9, moved=2 * 10**6
    )(window, *matrices)

    outgoing = call(
        patch_kernel,
        float_of(patch_count, layers, tile, win_size),
        [SMEM_SPEC] + [VMEM_SPEC] * 9,
        scratch=[pltpu.VMEM((layers, patch_count * tile, win_size), jnp.float32)],
        flops=10**10,
        moved=8 * 10**6,
    )(rows, received, observed[0], amplitude, object_re, object_im, *matrices)
    returned = lax.all_to_all(outgoing, "patch", split_axis=0, concat_axis=0, tiled=True)

    pieces = float_of(frame_count // 2, layers, tile, width)
    keep, send = call(
        add_kernel,
        (pieces, pieces),
        [SMEM_SPEC, SMEM_SPEC, VMEM_SPEC],
        scratch=[pltpu.VMEM((layers, tile, screen_cols), jnp.float32)],
        moved=8 * 10**6,
    )(cols, frame_id.reshape(1).astype(jnp.int32), returned)
    return frame_total(keep, send, frame_id)


def solution(mesh):
    in_specs = (P(None, "patch", None), P(), P(), P(), P(None, "patch"), P("frame", None, "patch"))
    out_specs = P(None, "patch", "frame")
    return jax.shard_map(body, mesh=mesh, in_specs=in_specs, out_specs=out_specs, check_vma=False)
```

time: 299 us -> 101 us (0.34); the launches traced: 295 us -> 100 us
  matrix products: 97.9 us -> 0 us
  local copies, waits for them, and re-layouts: 45.8 us -> 3.38 us
  blocking collectives: 0 us -> 33 us
  loops' own time: 29.2 us -> 0 us
  waiting for transfers between devices: 59.2 us -> 33.6 us
  other arithmetic: 17.7 us -> 1.23 us
  starting transfers between devices: 30.2 us -> 14.8 us
  between operations: 14.9 us -> 0.2 us
  Pallas kernels: 0 us -> 14.1 us
    dot_general x46 -> x0, matrix products: 97.9 us -> none  [matmul_high(): jnp.dot(left_op, right_op, precision=lax.Precision.HIGHEST, preferred_ele...]
    all_to_all x0 -> x1, blocking collectives: none -> 33 us  [body(): lax.all_to_all(outgoing, 'patch', split_axis=0, concat_axis=0, tiled=True)]
    reduce_scatter x1 -> x0, waiting for transfers between devices: 30.9 us -> none  [frame_total(): return lax.psum_scatter(values, 'frame', scatter_dimension=2, tiled=True)]
    another operation x2 -> x0, loops' own time: 29.2 us -> none  [the longest x1 29.1 us: body(): summed = lax.fori_loop(0, patch_count, add_band, jnp.zeros_like(screens))]
    ppermute x2 -> x4, waiting for transfers between devices: 2.6 us -> 24.3 us  [the longest x2 15.1 us: frame_total(): lax.ppermute(send, 'frame', [(i, i ^ step) for i in range(count)])]
    all_to_all x2 -> x1, starting transfers between devices: 23.8 us -> 7.25 us  [body(): lax.all_to_all(bands, 'patch', split_axis=0, concat_axis=0, tiled=True)]
    all_to_all x2 -> x1, waiting for transfers between devices: 25.7 us -> 9.37 us  [body(): lax.all_to_all(bands, 'patch', split_axis=0, concat_axis=0, tiled=True)]
    pallas_call x0 -> x4, Pallas kernels: none -> 14.1 us  [the longest x1 8.19 us: body(): call(patch_kernel, float_of(patch_count, layers, tile, win_size), [SMEM_S...]
  transfers between devices with their start and end apart: 5 -> 5, of which waited for: 4 -> 5; matrix products, arithmetic and copies ran while one was open for 11% -> 1% of each run, Pallas kernels for 0% -> 1%
where the time goes in v1:
time: 101 us; the launch traced here: 100 us
  waiting for transfers between devices  33.6 us (33%)
  blocking collectives  33 us (33%)
  starting transfers between devices  14.8 us (15%)
  Pallas kernels  14.1 us (14%)
  local copies, waits for them, and re-layouts  3.38 us (3%)
  other arithmetic  1.23 us (1%)
    all_to_all x1, blocking collectives, body(): lax.all_to_all(outgoing, 'patch', split_axis=0, concat_axis=0, tiled=True)  33 us
    ppermute x2, waiting for transfers between devices, frame_total(): lax.ppermute(send, 'frame', [(i, i ^ step) for i in range(count)])  15.1 us
    all_to_all x1, waiting for transfers between devices, body(): lax.all_to_all(bands, 'patch', split_axis=0, concat_axis=0, tiled=True)  9.37 us
    pallas_call x1, Pallas kernels, body(): call(patch_kernel, float_of(patch_count, layers, tile, win_size), [SMEM_S...  8.19 us
    ppermute x1, waiting for transfers between devices, body(): right = lax.ppermute(head, 'patch', [(i + 1, i) for i in range(ends)])  8.18 us
    all_to_all x1, starting transfers between devices, body(): lax.all_to_all(bands, 'patch', split_axis=0, concat_axis=0, tiled=True)  7.25 us
    ppermute x1, starting transfers between devices, body(): left = lax.ppermute(tail, 'patch', [(i, i + 1) for i in range(ends)])  4.56 us
    pallas_call x1, Pallas kernels, body(): call(cut_kernel, float_of(patch_count, layers, tile, win_size), [SMEM_SPE...  2.61 us
  transfers between devices with their start and end apart: 5, of which 5 were waited for; matrix products, arithmetic and copies ran while one was open for 1% of the time, Pallas kernels for 1%

profile of v1, /device:TPU:0, one launch (start us, length us, event | category | flops | bytes accessed | tf_op | source)
XLA Modules:
  0.0 100.2 jit_solution(6999147300456004638)
XLA Ops:
  0.0 0.0 copy-start
  0.0 0.7 copy-done
  0.7 0.0 copy-start.1
  0.7 1.6 %copy-done.1 = f32[2,64,4096]{2,1,0:T(8,128)S(1)} copy-done((f32[2,64,4096]{2,1,0:T(8,128)S(1)}, f32[2,64,4096]{2,1,0:T(8,128)}, u32[]{:S(2)}) %copy-start.1) | copy-done | bytes 2097176
  2.3 0.0 copy-start.8
  2.3 2.6 %shard_map.100 = f32[8,2,64,256]{3,2,1,0:T(8,128)} custom-call(s32[2,8]{1,0:T(2,128)S(1)} %dynamic-slice_bitcast_fusion.cols_ref, f32[2,64,4096]{2,1,0:T(8,128)S(1)} %copy-done.1), custom_call_target="tpu_custom_call" | custom-call | bytes 4194304 | tf_op jit(solution)/shard_map/pallas_call | solution.py:351
  4.9 7.3 %all-to-all-start = ((f32[8,2,64,256]{3,2,1,0:T(8,128)}), f32[8,2,64,256]{3,2,1,0:T(8,128)S(1)}, u32[]{:S(2)}, u32[]{:S(2)}) async-start(f32[8,2,64,256]{3,2,1,0:T(8,128)} %shard_map.100), calls=%async_computation | async-start | bytes 2097152 | tf_op jit(solution)/shard_map/all_to_all | solution.py:357
  12.1 0.0 copy-done.8
  12.1 0.1 fusion.1
  12.3 1.3 %collective-permute-start = (f32[384,64]{1,0:T(8,128)S(1)}, f32[384,64]{1,0:T(8,128)S(1)}, u32[]{:S(2)}, u32[]{:S(2)}) collective-permute-start(f32[384,64]{1,0:T(8,128)S(1)} %get-tuple-element.13), channel_id=1, source_target_pairs={{4,0},{8,4},{12,8},{16,12},{20,16},{24,20},{28,24},{5,1},{9,5},{13... | collective-permute-start | bytes 294920 | tf_op jit(solution)/shard_map/ppermute | solution.py:362
  13.6 4.6 %collective-permute-start.1 = (f32[384,64]{1,0:T(8,128)S(1)}, f32[384,64]{1,0:T(8,128)S(1)}, u32[]{:S(2)}, u32[]{:S(2)}) collective-permute-start(f32[384,64]{1,0:T(8,128)S(1)} %get-tuple-element.14), channel_id=1, source_target_pairs={{0,4},{4,8},{8,12},{12,16},{16,20},{20,24},{24,28},{1,5},{5,9},{9,... | collective-permute-start | bytes 294920 | tf_op jit(solution)/shard_map/ppermute | solution.py:363
  18.1 0.9 dynamic-slice_reduce_fusion.rows_ref
  19.0 0.0 copy-start.4
  19.0 0.0 copy-start.5
  19.0 0.0 copy-start.6
  19.0 0.0 copy-start.7
  19.0 8.2 %collective-permute-done = f32[384,64]{1,0:T(8,128)S(1)} collective-permute-done((f32[384,64]{1,0:T(8,128)S(1)}, f32[384,64]{1,0:T(8,128)S(1)}, u32[]{:S(2)}, u32[]{:S(2)}) %collective-permute-start) | collective-permute-done | bytes 98336 | tf_op jit(solution)/shard_map/ppermute | solution.py:362
  27.2 1.0 %collective-permute-done.1 = f32[384,64]{1,0:T(8,128)S(1)} collective-permute-done((f32[384,64]{1,0:T(8,128)S(1)}, f32[384,64]{1,0:T(8,128)S(1)}, u32[]{:S(2)}, u32[]{:S(2)}) %collective-permute-start.1) | collective-permute-done | bytes 98336 | tf_op jit(solution)/shard_map/ppermute | solution.py:363
  28.2 0.1 pad_maximum_fusion.2
  28.4 0.1 fusion.window_ref
  28.5 0.0 copy-done.4
  28.5 0.0 copy-done.5
  28.5 0.0 copy-done.6
  28.5 0.0 copy-done.7
  28.5 0.0 copy-start.2
  28.5 0.0 copy-start.3
  28.5 1.4 %shard_map.101 = (f32[256,384]{1,0:T(8,128)S(1)}, f32[256,384]{1,0:T(8,128)S(1)}) custom-call(f32[384,384]{1,0:T(8,128)S(1)} %fusion.window_ref, bf16[256,256]{1,0:T(8,128)(2,1)S(1)} %copy-done.7, bf16[256,256]{1,0:T(8,128)(2,1)S(1)} %copy-done.6, bf16[256,256]{1,0:T(8,128)(2,1)S(1)} %copy-done.5, bf16[256,256]{1,0:T(8,128)(2,1)S(1)} %copy-done.4), custom_call_target="tpu_custom_call" | custom-call | flops 3000000000 | bytes 2000000 | tf_op jit(solution)/shard_map/pallas_call | solution.py:367
  30.0 9.4 %all-to-all-done.bands_ref = f32[8,2,64,256]{3,2,1,0:T(8,128)S(1)} async-done(((f32[8,2,64,256]{3,2,1,0:T(8,128)}), f32[8,2,64,256]{3,2,1,0:T(8,128)S(1)}, u32[]{:S(2)}, u32[]{:S(2)}) %all-to-all-start) | async-done | bytes 1048608 | tf_op jit(solution)/shard_map/all_to_all | solution.py:357
  39.3 0.0 copy-done.2
  39.3 0.0 copy-done.3
  39.3 8.2 %shard_map.102 = f32[8,2,64,256]{3,2,1,0:T(8,128)S(1)} custom-call(s32[2]{0:T(128)S(1)} %dynamic-slice_reduce_fusion.rows_ref, f32[8,2,64,256]{3,2,1,0:T(8,128)S(1)} %all-to-all-done.bands_ref, f32[256,256]{1,0:T(8,128)S(1)} %bitcast.6, f32[256,256]{1,0:T(8,128)S(1)} %copy-done.3, f32[256,384]{1,0:T(8,128)S(1)} %get-tuple-element.9.ore_ref, ...), custom_call_target="tpu_custom_call" | custom-call | flops 10000000000 | bytes 8000000 | tf_op jit(solution)/shard_map/pallas_call | solution.py:371
  47.5 33.0 %all_to_all.10.bands_ref = f32[8,2,64,256]{3,2,1,0:T(8,128)S(1)} all-to-all(f32[8,2,64,256]{3,2,1,0:T(8,128)S(1)} %shard_map.102), channel_id=1, replica_groups=mesh['patch'=8,'frame'=4] {'patch'}, dimensions={0} | all-to-all | bytes 2097152 | tf_op jit(solution)/shard_map/all_to_all | solution.py:379
  80.5 1.9 %shard_map.103 = (f32[2,2,64,1024]{3,2,1,0:T(8,128)S(1)}, f32[2,2,64,1024]{3,2,1,0:T(8,128)S(1)}) custom-call(s32[2,8]{1,0:T(2,128)S(1)} %dynamic-slice_bitcast_fusion.cols_ref, s32[1]{0:T(128)} %bitcast.1.frame_ref, f32[8,2,64,256]{3,2,1,0:T(8,128)S(1)} %all_to_all.10.bands_ref), custom_call_target="tpu_custom_call" | custom-call | bytes 8000000 | tf_op jit(solution)/shard_map/pallas_call | solution.py:382
  82.4 0.1 collective-permute-start.2
  82.5 2.6 %collective-permute-done.2 = f32[2,2,64,1024]{3,2,1,0:T(8,128)S(1)} collective-permute-done((f32[2,2,64,1024]{3,2,1,0:T(8,128)S(1)}, f32[2,2,64,1024]{3,2,1,0:T(8,128)S(1)}, u32[]{:S(2)}, u32[]{:S(2)}) %collective-permute-start.2) | collective-permute-done | bytes 1048608 | tf_op jit(solution)/shard_map/ppermute | solution.py:326
  85.1 0.2 add.29
  85.3 1.6 %collective-permute-start.3 = (f32[1,2,64,1024]{3,2,1,0:T(8,128)S(1)}, f32[1,2,64,1024]{3,2,1,0:T(8,128)S(1)}, u32[]{:S(2)}, u32[]{:S(2)}) collective-permute-start(f32[1,2,64,1024]{3,2,1,0:T(8,128)S(1)} %constant_dynamic-slice_fusion), channel_id=1, source_target_pairs={{0,2},{1,3},{2,0},{3,1},{4,6},{5,7},{6,4},{7,5},{8,10},{9,11},{10,... | collective-permute-start | bytes 1572872 | tf_op jit(solution)/shard_map/ppermute | solution.py:326
  86.9 12.5 %collective-permute-done.3 = f32[1,2,64,1024]{3,2,1,0:T(8,128)S(1)} collective-permute-done((f32[1,2,64,1024]{3,2,1,0:T(8,128)S(1)}, f32[1,2,64,1024]{3,2,1,0:T(8,128)S(1)}, u32[]{:S(2)}, u32[]{:S(2)}) %collective-permute-start.3) | collective-permute-done | bytes 524320 | tf_op jit(solution)/shard_map/ppermute | solution.py:326
  99.4 0.9 add_bitcast_fusion
  (3 shorter events, 0.1 us)
Async XLA Ops:
  0.0 0.7 copy-start
  0.7 1.6 %copy-start.1 = (f32[2,64,4096]{2,1,0:T(8,128)S(1)}, f32[2,64,4096]{2,1,0:T(8,128)}, u32[]{:S(2)}) copy-start(f32[2,64,4096]{2,1,0:T(8,128)} %screens_ref.1) | copy-start | bytes 6291460
  2.3 9.9 %copy-start.8 = (f32[384,256]{1,0:T(8,128)S(1)}, f32[384,256]{1,0:T(8,128)}, u32[]{:S(2)}) copy-start(f32[384,256]{1,0:T(8,128)} %param.14) | copy-start | bytes 1179652
  4.9 34.4 %all-to-all-start = ((f32[8,2,64,256]{3,2,1,0:T(8,128)}), f32[8,2,64,256]{3,2,1,0:T(8,128)S(1)}, u32[]{:S(2)}, u32[]{:S(2)}) async-start(f32[8,2,64,256]{3,2,1,0:T(8,128)} %shard_map.100), calls=%async_computation | async-start | bytes 2097152 | tf_op jit(solution)/shard_map/all_to_all | solution.py:357
  12.3 15.0 %collective-permute-start = (f32[384,64]{1,0:T(8,128)S(1)}, f32[384,64]{1,0:T(8,128)S(1)}, u32[]{:S(2)}, u32[]{:S(2)}) collective-permute-start(f32[384,64]{1,0:T(8,128)S(1)} %get-tuple-element.13), channel_id=1, source_target_pairs={{4,0},{8,4},{12,8},{16,12},{20,16},{24,20},{28,24},{5,1},{9,5},{13... | collective-permute-start | bytes 294920 | tf_op jit(solution)/shard_map/ppermute | solution.py:362
  13.6 14.7 %collective-permute-start.1 = (f32[384,64]{1,0:T(8,128)S(1)}, f32[384,64]{1,0:T(8,128)S(1)}, u32[]{:S(2)}, u32[]{:S(2)}) collective-permute-start(f32[384,64]{1,0:T(8,128)S(1)} %get-tuple-element.14), channel_id=1, source_target_pairs={{0,4},{4,8},{8,12},{12,16},{16,20},{20,24},{24,28},{1,5},{5,9},{9,... | collective-permute-start | bytes 294920 | tf_op jit(solution)/shard_map/ppermute | solution.py:363
  19.0 9.5 %copy-start.4 = (bf16[256,256]{1,0:T(8,128)(2,1)S(1)}, bf16[256,256]{1,0:T(8,128)(2,1)}, u32[]{:S(2)}) copy-start(bf16[256,256]{1,0:T(8,128)(2,1)} %constant.62.clone.tl) | copy-start | bytes 393220
  19.0 9.5 %copy-start.5 = (bf16[256,256]{1,0:T(8,128)(2,1)S(1)}, bf16[256,256]{1,0:T(8,128)(2,1)}, u32[]{:S(2)}) copy-start(bf16[256,256]{1,0:T(8,128)(2,1)} %constant.61.clone.th) | copy-start | bytes 393220
  19.0 9.5 %copy-start.6 = (bf16[256,256]{1,0:T(8,128)(2,1)S(1)}, bf16[256,256]{1,0:T(8,128)(2,1)}, u32[]{:S(2)}) copy-start(bf16[256,256]{1,0:T(8,128)(2,1)} %constant.60.clone.fl) | copy-start | bytes 393220
  19.0 9.5 %copy-start.7 = (bf16[256,256]{1,0:T(8,128)(2,1)S(1)}, bf16[256,256]{1,0:T(8,128)(2,1)}, u32[]{:S(2)}) copy-start(bf16[256,256]{1,0:T(8,128)(2,1)} %constant.59.clone.fh) | copy-start | bytes 393220
  28.5 10.8 %copy-start.2 = (f32[1,256,256]{2,1,0:T(8,128)S(1)}, f32[1,256,256]{2,1,0:T(8,128)}, u32[]{:S(2)}) copy-start(f32[1,256,256]{2,1,0:T(8,128)} %param.15) | copy-start | bytes 786436
  28.5 10.8 %copy-start.3 = (f32[256,256]{1,0:T(8,128)S(1)}, f32[256,256]{1,0:T(8,128)}, u32[]{:S(2)}) copy-start(f32[256,256]{1,0:T(8,128)} %amplitude_ref.1) | copy-start | bytes 786436
  82.4 2.7 %collective-permute-start.2 = (f32[2,2,64,1024]{3,2,1,0:T(8,128)S(1)}, f32[2,2,64,1024]{3,2,1,0:T(8,128)S(1)}, u32[]{:S(2)}, u32[]{:S(2)}) collective-permute-start(f32[2,2,64,1024]{3,2,1,0:T(8,128)S(1)} %get-tuple-element.12), channel_id=1, source_target_pairs={{0,1},{1,0},{2,3},{3,2},{4,5},{5,4},{6,7},{7,6},{8,9},{9,8},{10,11... | collective-permute-start | bytes 3145736 | tf_op jit(solution)/shard_map/ppermute | solution.py:326
  85.3 14.0 %collective-permute-start.3 = (f32[1,2,64,1024]{3,2,1,0:T(8,128)S(1)}, f32[1,2,64,1024]{3,2,1,0:T(8,128)S(1)}, u32[]{:S(2)}, u32[]{:S(2)}) collective-permute-start(f32[1,2,64,1024]{3,2,1,0:T(8,128)S(1)} %constant_dynamic-slice_fusion), channel_id=1, source_target_pairs={{0,2},{1,3},{2,0},{3,1},{4,6},{5,7},{6,4},{7,5},{8,10},{9,11},{10,... | collective-permute-start | bytes 1572872 | tf_op jit(solution)/shard_map/ppermute | solution.py:326

commit v2 on v1

--- a/solution.py
+++ b/solution.py
@@ -301,10 +301,114 @@
 
     bit = frame_ref[0] & 1
     for chunk in range(chunks):
+        absolute = chunk ^ (frame_ref[0] // 2)
         for ref, low in ((keep_ref, bit), (send_ref, 1 - bit)):
-            begin = pl.multiple_of((2 * chunk + low) * width, LANES)
+            begin = pl.multiple_of((2 * absolute + low) * width, LANES)
             for layer in range(layers):
                 ref[chunk, layer] = sheet[layer, :, pl.ds(begin, width)]
+
+
+def greet(axis, peers):
+    barrier = pltpu.get_barrier_semaphore()
+    for peer in peers:
+        pl.semaphore_signal(
+            barrier, inc=1, device_id={axis: peer}, device_id_type=pl.DeviceIdType.MESH
+        )
+    pl.semaphore_wait(barrier, len(peers))
+
+
+def remote(source, target, send_sem, recv_sem, axis, peer):
+    return pltpu.make_async_remote_copy(
+        src_ref=source,
+        dst_ref=target,
+        send_sem=send_sem,
+        recv_sem=recv_sem,
+        device_id={axis: peer},
+        device_id_type=pl.DeviceIdType.MESH,
+    )
+
+
+def far_first(count):
+    return sorted(range(1, count), key=lambda step: -min(step, count - step))
+
+
+def exchange(count, in_ref, out_ref, send_sem, recv_sem, own_sem, edges=()):
+    me = lax.axis_index("patch")
+    steps = far_first(count)
+    peers = {step: lax.rem(me + step, count) for step in steps}
+    greet("patch", [peers[step] for step in steps])
+    copies = []
+    for number, (source, target, step) in enumerate(edges):
+        place = count + number
+        copies.append(
+            remote(source, target, send_sem.at[place], recv_sem.at[place], "patch", peers[step])
+        )
+    for step in steps:
+        copies.append(
+            remote(
+                in_ref.at[peers[step]],
+                out_ref.at[me],
+                send_sem.at[step],
+                recv_sem.at[step],
+                "patch",
+                peers[step],
+            )
+        )
+    own = pltpu.make_async_copy(in_ref.at[me], out_ref.at[me], own_sem)
+    for copy in copies:
+        copy.start()
+    own.start()
+    for copy in copies:
+        copy.wait()
+    own.wait()
+
+
+def forward_kernel(
+    count, in_ref, head_ref, tail_ref, out_ref, right_ref, left_ref, send_sem, recv_sem, own_sem
+):
+    edges = ((tail_ref, left_ref, 1), (head_ref, right_ref, count - 1))
+    exchange(count, in_ref, out_ref, send_sem, recv_sem, own_sem, edges)
+
+
+def return_kernel(count, in_ref, out_ref, send_sem, recv_sem, own_sem):
+    exchange(count, in_ref, out_ref, send_sem, recv_sem, own_sem)
+
+
+def frame_kernel(count, keep_ref, send_ref, out_ref, total, near, distant, *sems):
+    near_send, near_recv, far_send, far_recv = sems
+    me = lax.axis_index("frame")
+    chunks, layers = keep_ref.shape[:2]
+    levels = count.bit_length() - 1
+    peers = [me + (1 << k) * (1 - 2 * lax.rem(me // (1 << k), 2)) for k in range(levels)]
+    greet("frame", peers)
+    zeros = {r: (r & -r).bit_length() for r in range(1, chunks)}
+    order = sorted(zeros, key=zeros.get) + [0]
+    first = {}
+    for r in order:
+        for layer in range(layers):
+            sems = (near_send.at[r, layer], near_recv.at[r, layer])
+            first[r, layer] = remote(
+                send_ref.at[r, layer], near.at[r, layer], *sems, "frame", peers[0]
+            )
+            first[r, layer].start()
+    later = {}
+    for r in order:
+        top = zeros.get(r, levels)
+        for layer in range(layers):
+            first[r, layer].wait()
+            value = keep_ref[r, layer] + near[r, layer]
+            for k in range(1, top):
+                later[r ^ (1 << (k - 1)), layer].wait()
+                value = value + distant[r ^ (1 << (k - 1)), layer]
+            if r == 0:
+                out_ref[layer] = value
+            else:
+                total[r, layer] = value
+                sems = (far_send.at[r, layer], far_recv.at[r, layer])
+                later[r, layer] = remote(
+                    total.at[r, layer], distant.at[r, layer], *sems, "frame", peers[top]
+                )
+                later[r, layer].start()
 
 
 def call(kernel, out_shape, specs, scratch=(), flops=0, moved=0):
@@ -319,19 +423,32 @@
     )
 
 
-def frame_total(keep, send, frame_id):
+def talk(kernel, out_shape, specs, out_spec, scratch, identity):
+    return pl.pallas_call(
+        kernel,
+        out_shape=out_shape,
+        in_specs=specs,
+        out_specs=jax.tree.map(lambda _: out_spec, out_shape),
+        scratch_shapes=list(scratch),
+        compiler_params=pltpu.CompilerParams(
+            vmem_limit_bytes=VMEM_LIMIT, collective_id=identity, has_side_effects=True
+        ),
+    )
+
+
+def frame_total(keep, send):
     count = lax.axis_size("frame")
-    step = 1
-    while True:
-        received = lax.ppermute(send, "frame", [(i, i ^ step) for i in range(count)])
-        total = keep + received
-        if total.shape[0] == 1:
-            return total[0]
-        step *= 2
-        bit = (frame_id // step) % 2
-        pairs = total.reshape((total.shape[0] // 2, 2) + total.shape[1:])
-        keep = lax.dynamic_index_in_dim(pairs, bit, 1, keepdims=False)
-        send = lax.dynamic_index_in_dim(pairs, 1 - bit, 1, keepdims=False)
+    chunks, layers = keep.shape[:2]
+    buffers = [pltpu.VMEM(keep.shape, jnp.float32)] * 3
+    sems = [pltpu.SemaphoreType.DMA((chunks, layers))] * 4
+    return talk(
+        functools.partial(frame_kernel, count),
+        jax.ShapeDtypeStruct(keep.shape[1:], jnp.float32),
+        [VMEM_SPEC] * 2,
+        VMEM_SPEC,
+        buffers + sems,
+        2,
+    )(keep, send)
 
 
 def body(screens, row_offsets, col_offsets, amplitude, object_strip, observed):
@@ -354,13 +471,25 @@
         [SMEM_SPEC, VMEM_SPEC],
         moved=2 * screens.size * 4,
     )(cols, screens)
-    received = lax.all_to_all(bands, "patch", split_axis=0, concat_axis=0, tiled=True)
-
-    ends = patch_count - 1
+    any_spec = pl.BlockSpec(memory_space=pl.ANY)
     head = lax.slice_in_dim(object_strip, 0, HALO, axis=1)
     tail = lax.slice_in_dim(object_strip, object_strip.shape[1] - HALO, None, axis=1)
-    right = lax.ppermute(head, "patch", [(i + 1, i) for i in range(ends)])
-    left = lax.ppermute(tail, "patch", [(i, i + 1) for i in range(ends)])
+    edge = float_of(extent, HALO)
+    exchange_scratch = [
+        pltpu.SemaphoreType.DMA((patch_count + 2,)),
+        pltpu.SemaphoreType.DMA((patch_count + 2,)),
+        pltpu.SemaphoreType.DMA,
+    ]
+    received, right, left = talk(
+        functools.partial(forward_kernel, patch_count),
+        (float_of(*bands.shape), edge, edge),
+        [any_spec] * 3,
+        any_spec,
+        exchange_scratch,
+        0,
+    )(bands, head, tail)
+    right = jnp.where(place == patch_count - 1, 0.0, right)
+    left = jnp.where(place == 0, 0.0, left)
     window = jnp.concatenate([object_strip, right, left], axis=1)
     window = jnp.concatenate([window[HALO:], window[:HALO]], axis=0)
     spectrum = float_of(2 * (extent // RADIX), extent)
@@ -376,7 +505,14 @@
         flops=10**10,
         moved=8 * 10**6,
     )(rows, received, observed[0], amplitude, object_re, object_im, *matrices)
-    returned = lax.all_to_all(outgoing, "patch", split_axis=0, concat_axis=0, tiled=True)
+    returned = talk(
+        functools.partial(return_kernel, patch_count),
+        float_of(*outgoing.shape),
+        [any_spec],
+        any_spec,
+        exchange_scratch,
+        1,
+    )(outgoing)
 
     pieces = float_of(frame_count // 2, layers, tile, width)
     keep, send = call(
@@ -386,7 +522,7 @@
         scratch=[pltpu.VMEM((layers, tile, screen_cols), jnp.float32)],
         moved=8 * 10**6,
     )(cols, frame_id.reshape(1).astype(jnp.int32), returned)
-    return frame_total(keep, send, frame_id)
+    return frame_total(keep, send)
 
 
 def solution(mesh):

time: 101 us -> 92.3 us (0.914)
  the two profiles are of different devices: /device:TPU:0 before, /device:TPU:14 now
where the time goes in v2:
time: 92.3 us; the launch traced here: 92.1 us
  Pallas kernels  86.4 us (94%)
  local copies, waits for them, and re-layouts  5.27 us (6%)
    pallas_call x1, Pallas kernels, body(): talk(functools.partial(forward_kernel, patch_count), (float_of(*bands.sha...  31.5 us
    pallas_call x1, Pallas kernels, body(): talk(functools.partial(return_kernel, patch_count), float_of(*outgoing.sh...  26.1 us
    pallas_call x1, Pallas kernels, frame_total(): talk(functools.partial(frame_kernel, count), jax.ShapeDtypeStruct(keep.sh...  15.9 us
    pallas_call x1, Pallas kernels, body(): call(patch_kernel, float_of(patch_count, layers, tile, win_size), [SMEM_S...  8.1 us
    unnamed x19, local copies, waits for them, and re-layouts  3.22 us
    pallas_call x1, Pallas kernels, body(): call(add_kernel, (pieces, pieces), [SMEM_SPEC, SMEM_SPEC, VMEM_SPEC], scr...  1.87 us

profile of v2, /device:TPU:14, one launch (start us, length us, event | category | flops | bytes accessed | tf_op | source)
XLA Modules:
  0.0 92.1 jit_solution(9427768620031868130)
XLA Ops:
  0.0 0.0 copy-start
  0.0 0.9 dynamic-slice_reduce_fusion.rows_ref
  0.9 0.0 copy-done
  0.9 1.1 %fusion.1 = (f32[384,64]{1,0:T(8,128)S(1)}, f32[384,64]{1,0:T(8,128)S(1)}) fusion(f32[384,256]{1,0:T(8,128)} %param.14), kind=kLoop, calls=%fused_computation.8 | loop fusion | bytes 393216 | tf_op jit(solution)/shard_map/slice | solution.py:476
  2.0 0.0 copy-start.1
  2.0 1.6 %copy-done.1 = f32[2,64,4096]{2,1,0:T(8,128)S(1)} copy-done((f32[2,64,4096]{2,1,0:T(8,128)S(1)}, f32[2,64,4096]{2,1,0:T(8,128)}, u32[]{:S(2)}) %copy-start.1) | copy-done | bytes 2097176
  3.6 0.0 copy-start.8
  3.6 1.6 %shard_map.100.in_ref = f32[8,2,64,256]{3,2,1,0:T(8,128)S(1)} custom-call(s32[2,8]{1,0:T(2,128)S(1)} %dynamic-slice_bitcast_fusion.cols_ref, f32[2,64,4096]{2,1,0:T(8,128)S(1)} %copy-done.1), custom_call_target="tpu_custom_call" | custom-call | bytes 4194304 | tf_op jit(solution)/shard_map/pallas_call | solution.py:468
  5.3 31.5 %shard_map.101 = (f32[8,2,64,256]{3,2,1,0:T(8,128)S(1)}, f32[384,64]{1,0:T(8,128)S(1)}, f32[384,64]{1,0:T(8,128)S(1)}) custom-call(f32[8,2,64,256]{3,2,1,0:T(8,128)S(1)} %shard_map.100.in_ref, f32[384,64]{1,0:T(8,128)S(1)} %get-tuple-element.20.head_ref, f32[384,64]{1,0:T(8,128)S(1)} %get-tuple-element.19.tail_ref), custom_call_target="tpu_custom_call" | custom-call | tf_op jit(solution)/shard_map/pallas_call | solution.py:483
  36.8 0.0 copy-done.8
  36.8 0.0 copy-start.4
  36.8 0.0 copy-start.5
  36.8 0.0 copy-start.6
  36.8 0.0 copy-start.7
  36.8 0.1 pad_maximum_fusion.2
  37.0 0.1 fusion.window_ref
  37.1 0.6 copy-done.4
  37.7 0.1 copy-done.5
  37.7 0.1 copy-done.6
  37.8 0.1 copy-done.7
  37.9 0.0 copy-start.2
  37.9 0.0 copy-start.3
  37.9 1.4 %shard_map.102 = (f32[256,384]{1,0:T(8,128)S(1)}, f32[256,384]{1,0:T(8,128)S(1)}) custom-call(f32[384,384]{1,0:T(8,128)S(1)} %fusion.window_ref, bf16[256,256]{1,0:T(8,128)(2,1)S(1)} %copy-done.7, bf16[256,256]{1,0:T(8,128)(2,1)S(1)} %copy-done.6, bf16[256,256]{1,0:T(8,128)(2,1)S(1)} %copy-done.5, bf16[256,256]{1,0:T(8,128)(2,1)S(1)} %copy-done.4), custom_call_target="tpu_custom_call" | custom-call | flops 3000000000 | bytes 2000000 | tf_op jit(solution)/shard_map/pallas_call | solution.py:496
  39.3 0.0 copy-done.2
  39.3 0.0 copy-done.3
  39.3 8.1 %shard_map.103.in_ref = f32[8,2,64,256]{3,2,1,0:T(8,128)S(1)} custom-call(s32[2]{0:T(128)S(1)} %dynamic-slice_reduce_fusion.rows_ref, f32[8,2,64,256]{3,2,1,0:T(8,128)S(1)} %get-tuple-element.12.bands_ref, f32[256,256]{1,0:T(8,128)S(1)} %bitcast.4, f32[256,256]{1,0:T(8,128)S(1)} %copy-done.3, f32[256,384]{1,0:T(8,128)S(1)} %get-tuple-element.15.ore_ref, ...), custom_call_target="tpu_custom_call" | custom-call | flops 10000000000 | bytes 8000000 | tf_op jit(solution)/shard_map/pallas_call | solution.py:500
  47.4 26.1 %shard_map.104.bands_ref = f32[8,2,64,256]{3,2,1,0:T(8,128)S(1)} custom-call(f32[8,2,64,256]{3,2,1,0:T(8,128)S(1)} %shard_map.103.in_ref), custom_call_target="tpu_custom_call" | custom-call | tf_op jit(solution)/shard_map/pallas_call | solution.py:508
  73.5 1.9 %shard_map.105 = (f32[2,2,64,1024]{3,2,1,0:T(8,128)S(1)}, f32[2,2,64,1024]{3,2,1,0:T(8,128)S(1)}) custom-call(s32[2,8]{1,0:T(2,128)S(1)} %dynamic-slice_bitcast_fusion.cols_ref, s32[1]{0:T(128)} %bitcast.1.frame_ref, f32[8,2,64,256]{3,2,1,0:T(8,128)S(1)} %shard_map.104.bands_ref), custom_call_target="tpu_custom_call" | custom-call | bytes 8000000 | tf_op jit(solution)/shard_map/pallas_call | solution.py:518
  75.4 15.9 %shard_map.106 = f32[2,64,1024]{2,1,0:T(8,128)S(1)} custom-call(f32[2,2,64,1024]{3,2,1,0:T(8,128)S(1)} %get-tuple-element.17.keep_ref, f32[2,2,64,1024]{3,2,1,0:T(8,128)S(1)} %get-tuple-element.18.send_ref), custom_call_target="tpu_custom_call" | custom-call | tf_op jit(solution)/shard_map/pallas_call | solution.py:444
  91.3 0.8 copy.12
  (3 shorter events, 0.1 us)
Async XLA Ops:
  0.0 0.9 copy-start
  2.0 1.6 %copy-start.1 = (f32[2,64,4096]{2,1,0:T(8,128)S(1)}, f32[2,64,4096]{2,1,0:T(8,128)}, u32[]{:S(2)}) copy-start(f32[2,64,4096]{2,1,0:T(8,128)} %screens_ref.1) | copy-start | bytes 6291460
  3.6 33.1 %copy-start.8 = (f32[384,256]{1,0:T(8,128)S(1)}, f32[384,256]{1,0:T(8,128)}, u32[]{:S(2)}) copy-start(f32[384,256]{1,0:T(8,128)} %param.14) | copy-start | bytes 1179652
  36.8 0.9 copy-start.4
  36.8 1.0 %copy-start.5 = (bf16[256,256]{1,0:T(8,128)(2,1)S(1)}, bf16[256,256]{1,0:T(8,128)(2,1)}, u32[]{:S(2)}) copy-start(bf16[256,256]{1,0:T(8,128)(2,1)} %constant.33.clone.th) | copy-start | bytes 393220
  36.8 1.0 %copy-start.6 = (bf16[256,256]{1,0:T(8,128)(2,1)S(1)}, bf16[256,256]{1,0:T(8,128)(2,1)}, u32[]{:S(2)}) copy-start(bf16[256,256]{1,0:T(8,128)(2,1)} %constant.32.clone.fl) | copy-start | bytes 393220
  36.8 1.1 %copy-start.7 = (bf16[256,256]{1,0:T(8,128)(2,1)S(1)}, bf16[256,256]{1,0:T(8,128)(2,1)}, u32[]{:S(2)}) copy-start(bf16[256,256]{1,0:T(8,128)(2,1)} %constant.31.clone.fh) | copy-start | bytes 393220
  37.9 1.4 %copy-start.2 = (f32[1,256,256]{2,1,0:T(8,128)S(1)}, f32[1,256,256]{2,1,0:T(8,128)}, u32[]{:S(2)}) copy-start(f32[1,256,256]{2,1,0:T(8,128)} %param.15) | copy-start | bytes 786436
  37.9 1.4 %copy-start.3 = (f32[256,256]{1,0:T(8,128)S(1)}, f32[256,256]{1,0:T(8,128)}, u32[]{:S(2)}) copy-start(f32[256,256]{1,0:T(8,128)} %amplitude_ref.1) | copy-start | bytes 786436
